TPU v7x, 512 devices: a whole 4x8x8 slice. The times are simulated.
512 devices in a mesh: ta: 8 (over y_lo, core), ha: 8 (over y_hi, x), wa: 8 (over z).
Axes of the slice: x: 4, y: 8 (y_hi: 2, y_lo: 4; y = y_hi * 4 + y_lo), z: 8, core: 2. Of those that a mesh axis runs over, the one named last changes fastest.
Arguments:
- queries: bfloat16 [96, 32, 32, 1536], P('ta', 'ha', 'wa'), may hold values from -200 to 200
- keys: bfloat16 [96, 32, 32, 1536], P('ta', 'ha', 'wa'), may hold values from -8 to 8
- values: bfloat16 [96, 32, 32, 1536], P('ta', 'ha', 'wa'), may hold values from -6 to 6
Outputs:
- attended: bfloat16 [96, 32, 32, 1536], P('ta', 'ha', 'wa')
All inputs are finite; a program needn't handle non-finite values.
Results may differ from a plain program's by a relative error of at most 0.0048.
Values may be sent and summed in bfloat16 or wider, within the bound.
A program may use at most 128 MiB of HBM per device.

v0:
```python
import jax
import jax.numpy as jnp
from jax import lax
from jax.sharding import PartitionSpec as P

HEAD_DIM = 128
TT = 6
TH = 4
TW = 4


def with_halo(x, sides, width):
    for axis, dim in sides:
        size, length = (lax.axis_size(axis), x.shape[dim])
        up = [(i, (i + 1) % size) for i in range(size - 1)]
        down = [(j, i) for i, j in up]
        last = lax.slice_in_dim(x, length - width, length, axis=dim)
        first = lax.slice_in_dim(x, 0, width, axis=dim)
        before = lax.ppermute(last, axis, up)
        after = lax.ppermute(first, axis, down)
        x = jnp.concatenate([before, x, after], axis=dim)
    return x


def time_rim(source):
    return with_halo(source, (("ta", 0),), TT)


def height_rim(source):
    return with_halo(source, (("ha", 1),), TH)


def width_rim(source):
    return with_halo(source, (("wa", 2),), TW)


def spread_plane(source):
    return width_rim(height_rim(source))


def inside(position, count, amount, margin):
    root = position * amount - margin
    places = root + jnp.arange(amount + 2 * margin, dtype=jnp.int32)
    return (places >= 0) & (places < amount * count)


def window(source, anchor):
    level, across, along = anchor
    piece = source[
        level * TT : level * TT + 3 * TT,
        across * TH : across * TH + 3 * TH,
        along * TW : along * TW + 3 * TW,
    ]
    return piece.reshape((27 * TT * TH * TW,) + piece.shape[3:])


def body(queries, keys, values):
    frames, height, breadth, width_all = queries.shape
    tiles_time = frames // TT
    tiles_rows = height // TH
    tiles_cols = breadth // TW
    tile_tokens = TT * TH * TW
    head_count = width_all // HEAD_DIM
    factor = HEAD_DIM ** (-0.5)
    joined = jnp.concatenate([keys, values], axis=3)
    padded = spread_plane(time_rim(joined))
    time_inside = inside(lax.axis_index("ta"), lax.axis_size("ta"), frames, TT)
    rows_inside = inside(lax.axis_index("ha"), lax.axis_size("ha"), height, TH)
    cols_inside = inside(lax.axis_index("wa"), lax.axis_size("wa"), breadth, TW)
    inside_mask = (
        time_inside[:, None, None] & rows_inside[None, :, None] & cols_inside[None, None, :]
    )
    anchors = [
        (level, across, along)
        for level in range(tiles_time)
        for across in range(tiles_rows)
        for along in range(tiles_cols)
    ]
    tile_count = len(anchors)
    query_tiles = queries.reshape(tiles_time, TT, tiles_rows, TH, tiles_cols, TW, width_all)
    query_tiles = query_tiles.transpose(0, 2, 4, 1, 3, 5, 6).reshape(
        tile_count, tile_tokens, width_all
    )
    mask_windows = jnp.stack([window(inside_mask, anchor) for anchor in anchors])

    def per_head(head_index):
        offset = head_index * HEAD_DIM
        key_part = lax.dynamic_slice_in_dim(padded, offset, HEAD_DIM, 3)
        value_part = lax.dynamic_slice_in_dim(padded, width_all + offset, HEAD_DIM, 3)
        key_windows = jnp.stack([window(key_part, anchor) for anchor in anchors])
        value_windows = jnp.stack([window(value_part, anchor) for anchor in anchors])
        query_part = lax.dynamic_slice_in_dim(query_tiles, offset, HEAD_DIM, 2)
        scores = (
            jnp.einsum("nqd,nkd->nqk", query_part, key_windows, preferred_element_type=jnp.float32)
            * factor
        )
        scores = jnp.where(mask_windows[:, None, :], scores, -1e30)
        highest = jnp.max(scores, axis=2, keepdims=True)
        raised = jnp.exp(scores - highest)
        totals = jnp.sum(raised, axis=2, keepdims=True)
        weights = raised.astype(jnp.bfloat16)
        blended = jnp.einsum(
            "nqk,nkd->nqd", weights, value_windows, preferred_element_type=jnp.float32
        )
        return (blended / totals).astype(jnp.bfloat16)

    per_heads = lax.map(per_head, jnp.arange(head_count, dtype=jnp.int32))
    result = per_heads.transpose(1, 2, 0, 3).reshape(
        tiles_time, tiles_rows, tiles_cols, TT, TH, TW, width_all
    )
    return result.transpose(0, 3, 1, 4, 2, 5, 6).reshape(frames, height, breadth, width_all)


def solution(mesh):
    placed = (P("ta", "ha", "wa", None), P("ta", "ha", "wa", None), P("ta", "ha", "wa", None))
    return jax.shard_map(
        body, mesh=mesh, in_specs=placed, out_specs=P("ta", "ha", "wa", None), check_vma=False
    )
```

profile of v0, /device:TPU:22, one launch (start us, length us, event | category | flops | bytes accessed | tf_op | source)
XLA Modules:
  0.0 478.7 jit_solution(16586473352656126484)
XLA Ops:
  5.1 3.6 collective-permute-start.1
  8.8 5.6 %collective-permute-done = bf16[6,4,4,3072]{3,2,1,0:T(4,128)(2,1)S(1)} collective-permute-done((bf16[6,4,4,3072]{3,2,1,0:T(4,128)(2,1)S(1)}, bf16[6,4,4,3072]{3,2,1,0:T(4,128)(2,1)S(1)}, u32[]{:S(2)}, u32[]{:S(2)}) %collective-permute-start) | collective-permute-done | bytes 589856 | tf_op jit(solution)/shard_map/ppermute | solution.py:19
  17.8 5.8 %collective-permute-start.2 = (bf16[24,4,4,3072]{3,2,1,0:T(4,128)(2,1)S(1)}, bf16[24,4,4,3072]{3,2,1,0:T(4,128)(2,1)S(1)}, u32[]{:S(2)}, u32[]{:S(2)}) collective-permute-start(bf16[24,4,4,3072]{3,2,1,0:T(4,128)(2,1)S(1)} %pad_maximum_fusion.2), channel_id=1, source_target_pairs={{0,8},{8,16},{16,24},{24,32},{32,40},{40,48},{48,56},{1,9},{9,17},... | collective-permute-start | bytes 7077896 | tf_op jit(solution)/shard_map/ppermute | solution.py:19
  25.6 95.0 %collective-permute-done.2 = bf16[24,4,4,3072]{3,2,1,0:T(4,128)(2,1)S(1)} collective-permute-done((bf16[24,4,4,3072]{3,2,1,0:T(4,128)(2,1)S(1)}, bf16[24,4,4,3072]{3,2,1,0:T(4,128)(2,1)S(1)}, u32[]{:S(2)}, u32[]{:S(2)}) %collective-permute-start.2) | collective-permute-done | bytes 2359328 | tf_op jit(solution)/shard_map/ppermute | solution.py:19
  120.6 10.4 %collective-permute-done.3 = bf16[24,4,4,3072]{3,2,1,0:T(4,128)(2,1)S(1)} collective-permute-done((bf16[24,4,4,3072]{3,2,1,0:T(4,128)(2,1)S(1)}, bf16[24,4,4,3072]{3,2,1,0:T(4,128)(2,1)S(1)}, u32[]{:S(2)}, u32[]{:S(2)}) %collective-permute-start.3) | collective-permute-done | bytes 2359328 | tf_op jit(solution)/shard_map/ppermute | solution.py:20
  131.0 6.3 %pad_maximum_fusion.1 = bf16[24,12,4,3072]{3,2,1,0:T(4,128)(2,1)} fusion(bf16[24,4,4,3072]{3,2,1,0:T(4,128)(2,1)S(1)} %collective-permute-done.3, bf16[6,4,4,3072]{3,2,1,0:T(4,128)(2,1)S(1)} %collective-permute-done.1, bf16[12,4,4,3072]{3,2,1,0:T(4,128)(2,1)S(1)} %constant_dynamic-update-slice_fusion, bf16[6,4,4,3072]{3,2,1,0:T(4,128)(2,1)S(1)} %collective-permute-done, ...), kind=kLoop, calls=%fused_computation.26 | loop fusion | flops 14155776 | bytes 14155776 | tf_op jit(solution)/shard_map/concatenate | solution.py:21
  137.3 7.1 %collective-permute-start.4 = (bf16[24,12,4,3072]{3,2,1,0:T(4,128)(2,1)}, bf16[24,12,4,3072]{3,2,1,0:T(4,128)(2,1)}, u32[]{:S(2)}, u32[]{:S(2)}) collective-permute-start(bf16[24,12,4,3072]{3,2,1,0:T(4,128)(2,1)} %pad_maximum_fusion.1), channel_id=1, source_target_pairs={{0,1},{1,2},{2,3},{3,4},{4,5},{5,6},{6,7},{8,9},{9,10},{10,11},{11... | collective-permute-start | bytes 21233672 | tf_op jit(solution)/shard_map/ppermute | solution.py:19
  152.6 141.2 %collective-permute-done.4 = bf16[24,12,4,3072]{3,2,1,0:T(4,128)(2,1)} collective-permute-done((bf16[24,12,4,3072]{3,2,1,0:T(4,128)(2,1)}, bf16[24,12,4,3072]{3,2,1,0:T(4,128)(2,1)}, u32[]{:S(2)}, u32[]{:S(2)}) %collective-permute-start.4) | collective-permute-done | bytes 7077920 | tf_op jit(solution)/shard_map/ppermute | solution.py:19
  293.8 7.0 %collective-permute-done.5 = bf16[24,12,4,3072]{3,2,1,0:T(4,128)(2,1)} collective-permute-done((bf16[24,12,4,3072]{3,2,1,0:T(4,128)(2,1)}, bf16[24,12,4,3072]{3,2,1,0:T(4,128)(2,1)}, u32[]{:S(2)}, u32[]{:S(2)}) %collective-permute-start.5) | collective-permute-done | bytes 7077920 | tf_op jit(solution)/shard_map/ppermute | solution.py:20
  300.8 33.4 %pad_maximum_fusion = bf16[24,12,12,3072]{3,2,1,0:T(8,128)(2,1)} fusion(bf16[24,12,4,3072]{3,2,1,0:T(4,128)(2,1)} %collective-permute-done.5, bf16[24,4,4,3072]{3,2,1,0:T(4,128)(2,1)} %copy-done.1, bf16[6,4,4,3072]{3,2,1,0:T(4,128)(2,1)} %copy-done.3, bf16[12,4,4,3072]{3,2,1,0:T(4,128)(2,1)S(1)} %constant_dynamic-update-slice_fusion, ...), kind=kLoop, calls=%fused_computation.25 | loop fusion | flops 148635648 | bytes 42467328 | tf_op jit(solution)/shard_map/concatenate | solution.py:21
  334.2 142.0 %while.12 = (s32[]{:T(128)}, bf16[12,2,96,128]{3,2,1,0:T(8,128)(2,1)}, pred[2,2592]{1,0:T(4,128)(4,1)S(1)}, s32[12]{0:T(128)S(1)}, bf16[2,96,1536]{2,1,0:T(8,128...) while((s32[]{:T(128)}, ...), condition=%wide.region_3.4_spmd, body=%wide.region_0.3_spmd.sunk | while | flops 259663488 | bytes 27387496 | solution.py:107
  335.3 2.8 constant_dynamic-slice_fusion.5
  343.2 2.8 fusion.40
  355.0 2.8 fusion.40
  358.9 2.8 constant_dynamic-slice_fusion.5
  366.9 2.8 fusion.40
  394.2 2.8 constant_dynamic-slice_fusion.5
  425.6 2.8 fusion.40
  429.5 2.9 constant_dynamic-slice_fusion.5
  441.4 2.9 constant_dynamic-slice_fusion.5
  453.4 2.9 constant_dynamic-slice_fusion.5
  461.4 2.8 fusion.40
  465.3 2.9 constant_dynamic-slice_fusion.5
  473.4 2.8 fusion.40
  (149 shorter events, 119.1 us)
Async XLA Ops:
  3.2 11.2 %collective-permute-start = (bf16[6,4,4,3072]{3,2,1,0:T(4,128)(2,1)S(1)}, bf16[6,4,4,3072]{3,2,1,0:T(4,128)(2,1)S(1)}, u32[]{:S(2)}, u32[]{:S(2)}) collective-permute-start(bf16[6,4,4,3072]{3,2,1,0:T(4,128)(2,1)S(1)} %get-tuple-element.101), channel_id=1, source_target_pairs={{0,64},{64,128},{128,192},{192,256},{256,320},{320,384},{384,448},... | collective-permute-start | bytes 1769480 | tf_op jit(solution)/shard_map/ppermute | solution.py:19
  5.1 11.0 %collective-permute-start.1 = (bf16[6,4,4,3072]{3,2,1,0:T(4,128)(2,1)S(1)}, bf16[6,4,4,3072]{3,2,1,0:T(4,128)(2,1)S(1)}, u32[]{:S(2)}, u32[]{:S(2)}) collective-permute-start(bf16[6,4,4,3072]{3,2,1,0:T(4,128)(2,1)S(1)} %get-tuple-element.102), channel_id=1, source_target_pairs={{64,0},{128,64},{192,128},{256,192},{320,256},{384,320},{448,384},... | collective-permute-start | bytes 1769480 | tf_op jit(solution)/shard_map/ppermute | solution.py:20
  14.4 116.6 %copy-start.2 = (bf16[6,4,4,3072]{3,2,1,0:T(4,128)(2,1)}, bf16[6,4,4,3072]{3,2,1,0:T(4,128)(2,1)S(1)}, u32[]{:S(2)}) copy-start(bf16[6,4,4,3072]{3,2,1,0:T(4,128)(2,1)S(1)} %collective-permute-done) | copy-start | bytes 1769476
  16.1 114.9 %copy-start.3 = (bf16[6,4,4,3072]{3,2,1,0:T(4,128)(2,1)}, bf16[6,4,4,3072]{3,2,1,0:T(4,128)(2,1)S(1)}, u32[]{:S(2)}) copy-start(bf16[6,4,4,3072]{3,2,1,0:T(4,128)(2,1)S(1)} %collective-permute-done.1) | copy-start | bytes 1769476
  17.8 102.8 %collective-permute-start.2 = (bf16[24,4,4,3072]{3,2,1,0:T(4,128)(2,1)S(1)}, bf16[24,4,4,3072]{3,2,1,0:T(4,128)(2,1)S(1)}, u32[]{:S(2)}, u32[]{:S(2)}) collective-permute-start(bf16[24,4,4,3072]{3,2,1,0:T(4,128)(2,1)S(1)} %pad_maximum_fusion.2), channel_id=1, source_target_pairs={{0,8},{8,16},{16,24},{24,32},{32,40},{40,48},{48,56},{1,9},{9,17},... | collective-permute-start | bytes 7077896 | tf_op jit(solution)/shard_map/ppermute | solution.py:19
  23.7 107.3 %collective-permute-start.3 = (bf16[24,4,4,3072]{3,2,1,0:T(4,128)(2,1)S(1)}, bf16[24,4,4,3072]{3,2,1,0:T(4,128)(2,1)S(1)}, u32[]{:S(2)}, u32[]{:S(2)}) collective-permute-start(bf16[24,4,4,3072]{3,2,1,0:T(4,128)(2,1)S(1)} %pad_maximum_fusion.2), channel_id=1, source_target_pairs={{8,0},{16,8},{24,16},{32,24},{40,32},{48,40},{56,48},{9,1},{17,9},... | collective-permute-start | bytes 7077896 | tf_op jit(solution)/shard_map/ppermute | solution.py:20
  131.0 6.3 %copy-start.1 = (bf16[24,4,4,3072]{3,2,1,0:T(4,128)(2,1)}, bf16[24,4,4,3072]{3,2,1,0:T(4,128)(2,1)S(1)}, u32[]{:S(2)}) copy-start(bf16[24,4,4,3072]{3,2,1,0:T(4,128)(2,1)S(1)} %collective-permute-done.3) | copy-start | bytes 7077892
  137.3 156.4 %collective-permute-start.4 = (bf16[24,12,4,3072]{3,2,1,0:T(4,128)(2,1)}, bf16[24,12,4,3072]{3,2,1,0:T(4,128)(2,1)}, u32[]{:S(2)}, u32[]{:S(2)}) collective-permute-start(bf16[24,12,4,3072]{3,2,1,0:T(4,128)(2,1)} %pad_maximum_fusion.1), channel_id=1, source_target_pairs={{0,1},{1,2},{2,3},{3,4},{4,5},{5,6},{6,7},{8,9},{9,10},{10,11},{11... | collective-permute-start | bytes 21233672 | tf_op jit(solution)/shard_map/ppermute | solution.py:19
  144.5 156.3 %collective-permute-start.5 = (bf16[24,12,4,3072]{3,2,1,0:T(4,128)(2,1)}, bf16[24,12,4,3072]{3,2,1,0:T(4,128)(2,1)}, u32[]{:S(2)}, u32[]{:S(2)}) collective-permute-start(bf16[24,12,4,3072]{3,2,1,0:T(4,128)(2,1)} %pad_maximum_fusion.1), channel_id=1, source_target_pairs={{1,0},{2,1},{3,2},{4,3},{5,4},{6,5},{7,6},{9,8},{10,9},{11,10},{12... | collective-permute-start | bytes 21233672 | tf_op jit(solution)/shard_map/ppermute | solution.py:20
  152.6 181.5 %copy-start.4 = (pred[2,2592]{1,0:T(4,128)(4,1)S(1)}, pred[2,2592]{1,0:T(4,128)(4,1)}, u32[]{:S(2)}) copy-start(pred[2,2592]{1,0:T(4,128)(4,1)} %pad_add_fusion) | copy-start | bytes 15556
  341.1 1.4 copy-start
  352.9 1.4 copy-start
  364.7 1.4 copy-start
  376.4 1.4 copy-start
  388.2 1.4 copy-start
  400.0 1.4 copy-start
  411.7 1.4 copy-start
  423.5 1.4 copy-start
  435.4 1.4 copy-start
  447.3 1.4 copy-start
  459.2 1.4 copy-start
  471.2 1.4 copy-start
where the time goes:
time: 480 us; the launch traced here: 479 us
  waiting for transfers between devices  261 us (54%)
  local copies, waits for them, and re-layouts  85.6 us (18%)
  matrix products  54.7 us (11%)
  other arithmetic  48.1 us (10%)
  starting transfers between devices  21.8 us (5%)
  loops' own time  7.43 us (2%)
    ppermute x3, waiting for transfers between devices, with_halo(): before = lax.ppermute(last, axis, up)  242 us
    concatenate x3, other arithmetic, with_halo(): x = jnp.concatenate([before, x, after], axis=dim)  41.4 us
    slice x13, local copies, waits for them, and re-layouts, window(): source[level * TT:level * TT + 3 * TT, across * TH:across * TH + 3 * TH,...  34.1 us
    dot_general x12, matrix products, per_head(): jnp.einsum('nqk,nkd->nqd', weights, value_windows, preferred_element_type...  33.2 us
    dot_general x12, matrix products, per_head(): jnp.einsum('nqd,nkd->nqk', query_part, key_windows, preferred_element_typ...  21.5 us
    ppermute x3, waiting for transfers between devices, with_halo(): after = lax.ppermute(first, axis, down)  19.1 us
    while x24, local copies, waits for them, and re-layouts  17 us
    ppermute x3, starting transfers between devices, with_halo(): before = lax.ppermute(last, axis, up)  14.9 us
  transfers between devices with their start and end apart: 6, of which 6 were waited for; matrix products, arithmetic and copies ran while one was open for 1% of the time, Pallas kernels for 0%

commit v1 on v0

v1 whole, which is shorter than its diff:
```python
import functools
import math

import jax
import jax.numpy as jnp
from jax import lax
from jax.experimental import pallas as pl
from jax.experimental.pallas import tpu as pltpu
from jax.sharding import PartitionSpec as P

HEAD_DIM = 128
TILE = 96
MESH = pl.DeviceIdType.MESH
SCALE = HEAD_DIM**-0.5 * math.log2(math.e)


def kernel(
    heads, q_hbm, kv_hbm, out_hbm,
    qb, kv, valid, osend, orecv, ssend, srecv, own_o, own_l, outb,
    lq, lkv, lout, xs, xr, ts, tr, qs, qr, os_, or_, ss, sr,
):
    t, h, w = lax.axis_index("ta"), lax.axis_index("ha"), lax.axis_index("wa")
    nt, nh, nw = lax.axis_size("ta"), lax.axis_size("ha"), lax.axis_size("wa")
    has_t = (t > 0, t < nt - 1)
    has_h = (h > 0, h < nh - 1)
    has_w = (w > 0, w < nw - 1)
    near_t = ((t - 1, h, w), (t + 1, h, w))
    near_h = ((t, h - 1, w), (t, h + 1, w))
    near_w = ((t, h, w - 1), (t, h, w + 1))

    def remote(src, dst, send, recv, device):
        return pltpu.make_async_remote_copy(src, dst, send, recv, device_id=device, device_id_type=MESH)

    def x_copy(j, d):
        return remote(kv_hbm.at[j], kv.at[j, 1:3, 0 if d else 2], xs.at[j, d], xr.at[j, 1 - d], near_h[d])

    def t_copy(j, d, hh):
        src = kv_hbm.at[j, d] if hh == 1 else kv.at[j, 1 + d, hh]
        return remote(src, kv.at[j, 0 if d else 3, hh], ts.at[j, d, hh], tr.at[j, 1 - d, hh], near_t[d])

    def q_copy(j, d):
        return remote(q_hbm.at[j], qb.at[j, :, 0 if d else 2], qs.at[j, d], qr.at[j, 1 - d], near_w[d])

    def o_copy(j, d):
        return remote(osend.at[j, d], orecv.at[j, 1 - d], os_.at[j, d], or_.at[j, 1 - d], near_w[d])

    def s_copy(j, d):
        return remote(ssend.at[j, d], srecv.at[j, 1 - d], ss.at[j, d], sr.at[j, 1 - d], near_w[d])

    def x_in(j, d):
        return remote(kv_hbm.at[j], kv.at[j, 1:3, 2 * d], xs.at[j, d], xr.at[j, d], near_h[d])

    def t_in(j, d, hh):
        return remote(kv_hbm.at[j, d], kv.at[j, 3 * d, hh], ts.at[j, d, hh], tr.at[j, d, hh], near_t[d])

    def q_in(j, d):
        return remote(q_hbm.at[j], qb.at[j, :, 2 * d], qs.at[j, d], qr.at[j, d], near_w[d])

    def o_in(j, d):
        return remote(osend.at[j, d], orecv.at[j, d], os_.at[j, d], or_.at[j, d], near_w[d])

    def s_in(j, d):
        return remote(ssend.at[j, d], srecv.at[j, d], ss.at[j, d], sr.at[j, d], near_w[d])

    def q_local(j):
        return pltpu.make_async_copy(q_hbm.at[j], qb.at[j, :, 1], lq.at[j])

    def kv_local(j):
        return pltpu.make_async_copy(kv_hbm.at[j], kv.at[j, 1:3, 1], lkv.at[j])

    def out_local(j):
        return pltpu.make_async_copy(outb.at[j], out_hbm.at[j], lout.at[j])

    barrier = pltpu.get_barrier_semaphore()
    count = jnp.int32(0)
    for has, near in ((has_t, near_t), (has_h, near_h), (has_w, near_w)):
        for d in (0, 1):
            pl.when(has[d])(
                lambda near=near, d=d: pl.semaphore_signal(
                    barrier, inc=1, device_id=near[d], device_id_type=MESH
                )
            )
            count += has[d].astype(jnp.int32)

    @pl.loop(0, heads)
    def _(j):
        kv_local(j).start()
        q_local(j).start()

    for tt in range(4):
        for hh in range(3):
            here = jnp.bool_(True)
            if tt in (0, 3):
                here = here & has_t[tt // 3]
            if hh in (0, 2):
                here = here & has_h[hh // 2]
            valid[tt, hh] = jnp.full((TILE, HEAD_DIM), here.astype(jnp.float32)).astype(jnp.bfloat16)
    for d in (0, 1):
        @pl.when(jnp.logical_not(has_w[d]))
        def _():
            qb[:, :, 2 * d] = jnp.zeros_like(qb[:, :, 2 * d])
            orecv[:, d] = jnp.zeros_like(orecv[:, d])
            srecv[:, d] = jnp.full_like(srecv[:, d], -1e30)

    pl.semaphore_wait(barrier, count)

    @pl.loop(0, heads)
    def _(j):
        for d in (0, 1):
            pl.when(has_h[d])(lambda: x_copy(j, d).start())
        for d in (0, 1):
            pl.when(has_t[d])(lambda: t_copy(j, d, 1).start())
        for d in (0, 1):
            pl.when(has_w[d])(lambda: q_copy(j, d).start())

    rows = lax.broadcasted_iota(jnp.int32, (TILE, HEAD_DIM), 0)
    lanes = lax.broadcasted_iota(jnp.int32, (TILE, HEAD_DIM), 1)
    diagonal = rows == lanes

    def forward(j):
        for e in (0, 1):
            @pl.when(has_h[e])
            def _():
                x_in(j, e).wait_recv()
                for d in (0, 1):
                    pl.when(has_t[d])(lambda: t_copy(j, d, 2 * e).start())

    def attend(j):
        kv_local(j).wait()
        q_local(j).wait()
        for d in (0, 1):
            pl.when(has_w[d])(lambda: q_in(j, d).wait_recv())
        for d in (0, 1):
            @pl.when(has_t[d])
            def _():
                t_in(j, d, 1).wait_recv()
                for e in (0, 1):
                    pl.when(has_h[e])(lambda: t_in(j, d, 2 * e).wait_recv())

        none = jnp.zeros((TILE, HEAD_DIM), jnp.bfloat16)
        for e in (0, 1):
            @pl.when(jnp.logical_not(has_h[e]))
            def _():
                for tt in range(4):
                    kv[j, tt, 2 * e, 0] = kv[j, 1 + tt // 2, 1, 0]
                    kv[j, tt, 2 * e, 1] = none
        for d in (0, 1):
            @pl.when(jnp.logical_not(has_t[d]))
            def _():
                for hh in range(3):
                    kv[j, 3 * d, hh, 0] = kv[j, 1 + d, 1, 0]
                    kv[j, 3 * d, hh, 1] = none

        for k in (0, 1):
            queries = qb[j, k].reshape(3 * TILE, HEAD_DIM)
            keys = kv[j, k : k + 3, :, 0].reshape(9 * TILE, HEAD_DIM)
            values = kv[j, k : k + 3, :, 1].reshape(9 * TILE, HEAD_DIM)
            counted = valid[k : k + 3].reshape(9 * TILE, HEAD_DIM)
            scores = lax.dot_general(
                queries, keys, (((1,), (1,)), ((), ())), preferred_element_type=jnp.float32
            )
            highest = jnp.max(scores, axis=1, keepdims=True)
            weights = jnp.exp2((scores - highest) * SCALE).astype(jnp.bfloat16)
            blended = jnp.dot(
                weights, jnp.concatenate([values, counted], axis=1), preferred_element_type=jnp.float32
            )
            totals = blended[:, HEAD_DIM:]
            part = blended[:, :HEAD_DIM] / totals
            level = highest * SCALE + jnp.log2(totals)
            own_o[j, k] = part[TILE : 2 * TILE]
            own_l[j, k] = level[TILE : 2 * TILE]
            for d in (0, 1):
                at = slice(2 * d * TILE, (2 * d + 1) * TILE)
                osend[j, d, k] = part[at].astype(jnp.bfloat16)
                ssend[j, d, k : k + 1] = jnp.sum(jnp.where(diagonal, level[at], 0.0), axis=0, keepdims=True)
        for d in (0, 1):
            @pl.when(has_w[d])
            def _():
                o_copy(j, d).start()
                s_copy(j, d).start()

    def combine(j):
        for d in (0, 1):
            @pl.when(has_w[d])
            def _():
                o_in(j, d).wait_recv()
                s_in(j, d).wait_recv()
        for k in (0, 1):
            levels = [own_l[j, k]]
            for d in (0, 1):
                row = jnp.broadcast_to(srecv[j, d, k : k + 1], (TILE, HEAD_DIM))
                levels.append(jnp.sum(jnp.where(diagonal, row, 0.0), axis=1, keepdims=True))
            top = jnp.maximum(jnp.maximum(levels[1], levels[2]), levels[0])
            shares = [jnp.exp2(level - top) for level in levels]
            mixed = shares[0] * own_o[j, k]
            for d in (0, 1):
                mixed += shares[1 + d] * orecv[j, d, k].astype(jnp.float32)
            outb[j, k] = (mixed / (shares[0] + shares[1] + shares[2])).astype(jnp.bfloat16)
        out_local(j).start()

    @pl.loop(0, heads + 2)
    def _(step):
        pl.when(step < heads)(lambda: forward(step))
        pl.when((step >= 1) & (step <= heads))(lambda: attend(step - 1))
        pl.when(step >= 2)(lambda: combine(step - 2))

    @pl.loop(0, heads)
    def _(j):
        out_local(j).wait()
        for d in (0, 1):
            @pl.when(has_h[d])
            def _():
                x_copy(j, d).wait_send()

            @pl.when(has_t[d])
            def _():
                t_copy(j, d, 1).wait_send()
                for e in (0, 1):
                    pl.when(has_h[e])(lambda: t_copy(j, d, 2 * e).wait_send())

            @pl.when(has_w[d])
            def _():
                q_copy(j, d).wait_send()
                o_copy(j, d).wait_send()
                s_copy(j, d).wait_send()


def body(queries, keys, values):
    frames, height, breadth, width_all = queries.shape
    heads = width_all // HEAD_DIM
    split = [x.reshape(2, TILE, heads, HEAD_DIM).transpose(2, 0, 1, 3) for x in (queries, keys, values)]
    pairs = jnp.stack(split[1:], axis=2)
    bf16, f32 = jnp.bfloat16, jnp.float32
    dma = pltpu.SemaphoreType.DMA
    result = pl.pallas_call(
        functools.partial(kernel, heads),
        out_shape=jax.ShapeDtypeStruct((heads, 2, TILE, HEAD_DIM), bf16),
        in_specs=[pl.BlockSpec(memory_space=pl.ANY)] * 2,
        out_specs=pl.BlockSpec(memory_space=pl.ANY),
        scratch_shapes=[
            pltpu.VMEM((heads, 2, 3, TILE, HEAD_DIM), bf16),
            pltpu.VMEM((heads, 4, 3, 2, TILE, HEAD_DIM), bf16),
            pltpu.VMEM((4, 3, TILE, HEAD_DIM), bf16),
            pltpu.VMEM((heads, 2, 2, TILE, HEAD_DIM), bf16),
            pltpu.VMEM((heads, 2, 2, TILE, HEAD_DIM), bf16),
            pltpu.VMEM((heads, 2, 8, HEAD_DIM), f32),
            pltpu.VMEM((heads, 2, 8, HEAD_DIM), f32),
            pltpu.VMEM((heads, 2, TILE, HEAD_DIM), f32),
            pltpu.VMEM((heads, 2, TILE, HEAD_DIM), f32),
            pltpu.VMEM((heads, 2, TILE, HEAD_DIM), bf16),
            dma((heads,)), dma((heads,)), dma((heads,)),
            dma((heads, 2)), dma((heads, 2)),
            dma((heads, 2, 3)), dma((heads, 2, 3)),
            dma((heads, 2)), dma((heads, 2)),
            dma((heads, 2)), dma((heads, 2)),
            dma((heads, 2)), dma((heads, 2)),
        ],
        compiler_params=pltpu.CompilerParams(
            collective_id=0, has_side_effects=True, vmem_limit_bytes=48 * 2**20
        ),
        name="window_attention",
    )(split[0], pairs)
    return result.transpose(1, 2, 0, 3).reshape(frames, height, breadth, width_all)


def solution(mesh):
    placed = (P("ta", "ha", "wa", None),) * 3
    return jax.shard_map(
        body, mesh=mesh, in_specs=placed, out_specs=P("ta", "ha", "wa", None), check_vma=False
    )
```

time: 480 us -> 112 us (0.23)
  the two profiles are of different devices: /device:TPU:22 before, /device:TPU:7 now
where the time goes in v1:
time: 112 us
  Pallas kernels  106 us (95%)
  local copies, waits for them, and re-layouts  5.4 us (5%)
    pallas_call x1, Pallas kernels, body(): pl.pallas_call(functools.partial(kernel, heads), out_shape=jax.ShapeDtype...  106 us
    reshape x4, local copies, waits for them, and re-layouts, body(): x.reshape(2, TILE, heads, HEAD_DIM).transpose(2, 0, 1, 3)  2.65 us

profile of v1, /device:TPU:7, one launch (start us, length us, event | category | flops | bytes accessed | tf_op | source)
XLA Modules:
  0.0 112.0 jit_solution(890962041496034261)
XLA Ops:
  0.0 0.0 copy-start
  0.0 1.7 %reshape.13 = bf16[2,96,12,128]{3,2,1,0:T(8,128)(2,1)S(1)} reshape(bf16[12,4,4,1536]{3,2,1,0:T(4,128)(2,1)} %param.4) | data formatting | bytes 1179648 | tf_op jit(solution)/shard_map/reshape | solution.py:231
  1.7 0.0 copy-done
  1.7 0.4 reshape.14
  2.1 0.3 copy_bitcast_fusion
  2.4 0.0 copy-start.1
  2.5 0.1 pad_maximum_fusion.kv_hbm
  2.6 0.9 copy-done.1
  3.5 0.4 reshape.12
  3.9 0.2 copy.11
  4.1 106.4 %window_attention.1 = bf16[12,2,96,128]{3,2,1,0:T(8,128)(2,1)S(1)} custom-call(bf16[12,2,96,128]{3,2,1,0:T(8,128)(2,1)S(1)} %bitcast.12, bf16[12,2,2,96,128]{4,3,2,1,0:T(8,128)(2,1)S(1)} %pad_maximum_fusion.kv_hbm), custom_call_target="tpu_custom_call" | custom-call | tf_op jit(solution)/shard_map/window_attention/pallas_call | solution.py:235
  110.5 0.4 copy.7
  110.9 1.1 reshape.15
Async XLA Ops:
  0.0 1.7 %copy-start = (bf16[12,4,4,1536]{3,2,1,0:T(4,128)(2,1)S(1)}, bf16[12,4,4,1536]{3,2,1,0:T(4,128)(2,1)}, u32[]{:S(2)}) copy-start(bf16[12,4,4,1536]{3,2,1,0:T(4,128)(2,1)} %param.5) | copy-start | bytes 1769476
  2.4 1.1 copy-start.1

commit v2 on v1

v2 whole, which is shorter than its diff:
```python
import functools
import math

import jax
import jax.numpy as jnp
from jax import lax
from jax.experimental import pallas as pl
from jax.experimental.pallas import tpu as pltpu
from jax.sharding import PartitionSpec as P

HEAD_DIM = 128
TT, TH, TW = 6, 4, 4
TILE = TT * TH * TW
MESH = pl.DeviceIdType.MESH
SCALE = HEAD_DIM**-0.5 * math.log2(math.e)
AHEAD = 3
BEHIND = 3


def kernel(
    heads, q_hbm, k_hbm, v_hbm, outb,
    q_own, k_own, v_own, qb, kv, valid, osend, orecv, ssend, srecv, own_o, own_l,
    passing, load, es, xs, xr, ts, tr, qs, qr, os_, or_, ss, sr, ps, pr, fs, fr,
):
    t, h, w = lax.axis_index("ta"), lax.axis_index("ha"), lax.axis_index("wa")
    nt, nh, nw = lax.axis_size("ta"), lax.axis_size("ha"), lax.axis_size("wa")
    has_t = (t > 0, t < nt - 1)
    has_h = (h > 0, h < nh - 1)
    has_w = (w > 0, w < nw - 1)
    near_t = ((t - 1, h, w), (t + 1, h, w))
    near_h = ((t, h - 1, w), (t, h + 1, w))
    near_w = ((t, h, w - 1), (t, h, w + 1))
    low, high = nh // 2 - 1, nh // 2
    far = (h == high, h == low)
    is_far = (h == low) | (h == high)
    is_relay = (h == 0) | (h == nh - 1)
    relay = (t, jnp.where(h == low, 0, nh - 1), w)
    other_relay = (t, jnp.where(h == low, nh - 1, 0), w)
    relay_from = (t, jnp.where(h == 0, low, high), w)
    relay_to = (t, jnp.where(h == 0, high, low), w)
    far_slot = jnp.where(h == low, 2, 0)
    relay_slot = jnp.where(h == 0, 0, 2)

    off = lax.rem(t, 2)
    has_off = (off == 0) & has_t[0] | (off == 1) & has_t[1]
    is_inner = (h == low - 1) | (h == high + 1)
    inner_slot = jnp.where(h == low - 1, 0, 2)
    inner_to = (t, jnp.where(h == low - 1, low, high), w)

    def remote(src, dst, send, recv, device):
        return pltpu.make_async_remote_copy(src, dst, send, recv, device_id=device, device_id_type=MESH)

    def x_copy(j, d):
        return remote(kv.at[j, 1:3, 1], kv.at[j, 1:3, 0 if d else 2], xs.at[j, d], xr.at[j, 1 - d], near_h[d])

    def x_half(j, d):
        return remote(
            kv.at[j, 1, 1], kv.at[j, 1, 0 if d else 2], xs.at[j, d], xr.at[j, 1 - d], near_h[d]
        )

    def to_relay(j):
        return remote(kv.at[j, 2, 1], passing.at[j], ps.at[j], pr.at[j], relay)

    def relay_in(j):
        return remote(kv.at[j, 2, 1], passing.at[j], ps.at[j], pr.at[j], relay_from)

    def relay_out(j):
        return remote(passing.at[j], kv.at[j, 2, relay_slot], fs.at[j], fr.at[j], relay_to)

    def from_relay(j):
        return remote(passing.at[j], kv.at[j, 2, far_slot], fs.at[j], fr.at[j], other_relay)

    def t_copy(j, d, hh):
        return remote(kv.at[j, 1 + d, hh], kv.at[j, 0 if d else 3, hh], ts.at[j, d, hh], tr.at[j, 1 - d, hh], near_t[d])

    def edge_copy(j):
        return remote(
            kv.at[j, 3 * off, 1], kv.at[j, 3 * off, inner_slot], es.at[j], tr.at[j, off, inner_slot], inner_to
        )

    def q_copy(j, d):
        return remote(qb.at[j, :, 1], qb.at[j, :, 0 if d else 2], qs.at[j, d], qr.at[j, 1 - d], near_w[d])

    def o_copy(j, d):
        return remote(osend.at[j, d], orecv.at[j, 1 - d], os_.at[j, d], or_.at[j, 1 - d], near_w[d])

    def s_copy(j, d):
        return remote(ssend.at[j, d], srecv.at[j, 1 - d], ss.at[j, d], sr.at[j, 1 - d], near_w[d])

    def x_in(j, d):
        return remote(kv.at[j, 1:3, 1], kv.at[j, 1:3, 2 * d], xs.at[j, d], xr.at[j, d], near_h[d])

    def x_half_in(j, d):
        return remote(kv.at[j, 1, 1], kv.at[j, 1, 2 * d], xs.at[j, d], xr.at[j, d], near_h[d])

    def t_in(j, d, hh):
        return remote(kv.at[j, 1 + d, 1], kv.at[j, 3 * d, hh], ts.at[j, d, hh], tr.at[j, d, hh], (t + 2 * d - 1, h, w))

    def q_in(j, d):
        return remote(qb.at[j, :, 1], qb.at[j, :, 2 * d], qs.at[j, d], qr.at[j, d], near_w[d])

    def o_in(j, d):
        return remote(osend.at[j, d], orecv.at[j, d], os_.at[j, d], or_.at[j, d], near_w[d])

    def s_in(j, d):
        return remote(ssend.at[j, d], srecv.at[j, d], ss.at[j, d], sr.at[j, d], near_w[d])

    loads = [
        pltpu.make_async_copy(src, dst, load.at[i])
        for i, (src, dst) in enumerate(((k_hbm, k_own), (v_hbm, v_own), (q_hbm, q_own)))
    ]
    for copy in loads:
        copy.start()

    barrier = pltpu.get_barrier_semaphore()
    count = jnp.int32(0)
    for has, near in ((has_t, near_t), (has_h, near_h), (has_w, near_w)):
        for d in (0, 1):
            pl.when(has[d])(
                lambda near=near, d=d: pl.semaphore_signal(
                    barrier, inc=1, device_id=near[d], device_id_type=MESH
                )
            )
            count += has[d].astype(jnp.int32)
    for here, near in ((is_far, relay), (is_far, other_relay), (is_relay, relay_from), (is_relay, relay_to)):
        pl.when(here)(
            lambda near=near: pl.semaphore_signal(barrier, inc=1, device_id=near, device_id_type=MESH)
        )
        count += here.astype(jnp.int32)

    for tt in range(4):
        for hh in range(3):
            here = jnp.bool_(True)
            if tt in (0, 3):
                here = here & has_t[tt // 3]
            if hh in (0, 2):
                here = here & has_h[hh // 2]
            valid[tt, hh] = jnp.full((TILE, HEAD_DIM), here.astype(jnp.float32)).astype(jnp.bfloat16)
    for d in (0, 1):
        @pl.when(jnp.logical_not(has_w[d]))
        def _():
            qb[:, :, 2 * d] = jnp.zeros_like(qb[:, :, 2 * d])
            orecv[:, d] = jnp.zeros_like(orecv[:, d])
            srecv[:, d] = jnp.full_like(srecv[:, d], -1e30)

    def tiles(ref, j):
        at = pl.ds(pl.multiple_of(j * HEAD_DIM, HEAD_DIM), HEAD_DIM)
        return ref[:, :, :, at].reshape(2, TILE, HEAD_DIM)

    for copy in loads:
        copy.wait()

    none = jnp.zeros((TILE, HEAD_DIM), jnp.bfloat16)

    @pl.loop(0, heads)
    def _(j):
        kv[j, 1:3, 1, 0] = tiles(k_own, j)
        kv[j, 1:3, 1, 1] = tiles(v_own, j)
        qb[j, :, 1] = tiles(q_own, j)
        for e in (0, 1):
            @pl.when(jnp.logical_not(has_h[e]))
            def _():
                for tt in range(4):
                    kv[j, tt, 2 * e, 0] = kv[j, 1 + tt // 2, 1, 0]
                    kv[j, tt, 2 * e, 1] = none
        for d in (0, 1):
            @pl.when(jnp.logical_not(has_t[d]))
            def _():
                for hh in range(3):
                    kv[j, 3 * d, hh, 0] = kv[j, 1 + d, 1, 0]
                    kv[j, 3 * d, hh, 1] = none

    pl.semaphore_wait(barrier, count)

    def launch(j):
        for d in (0, 1):
            @pl.when(far[d])
            def _():
                to_relay(j).start()
                x_half(j, d).start()

            pl.when(has_h[d] & jnp.logical_not(far[d]))(lambda: x_copy(j, d).start())
        for d in (0, 1):
            pl.when(has_t[d])(lambda: t_copy(j, d, 1).start())
        for d in (0, 1):
            pl.when(has_w[d])(lambda: q_copy(j, d).start())

    pl.loop(0, AHEAD)(launch)

    rows = lax.broadcasted_iota(jnp.int32, (TILE, HEAD_DIM), 0)
    lanes = lax.broadcasted_iota(jnp.int32, (TILE, HEAD_DIM), 1)
    diagonal = rows == lanes

    def spreads(d, e):
        return has_t[d] & jnp.logical_not((off == d) & far[1 - e])

    def forward(j):
        @pl.when(is_relay)
        def _():
            relay_in(j).wait_recv()
            relay_out(j).start()

        @pl.when(is_inner & has_off)
        def _():
            t_in(j, off, 1).wait_recv()
            edge_copy(j).start()

        def spread(e):
            for d in (0, 1):
                pl.when(spreads(d, e))(lambda: t_copy(j, d, 2 * e).start())

        for e in (0, 1):
            @pl.when(has_h[e] & jnp.logical_not(far[e]))
            def _():
                x_in(j, e).wait_recv()
                spread(e)
        for e in (0, 1):
            @pl.when(far[e])
            def _():
                x_half_in(j, e).wait_recv()
                from_relay(j).wait_recv()
                spread(e)

    def attend(j):
        for d in (0, 1):
            pl.when(has_w[d])(lambda: q_in(j, d).wait_recv())
        for d in (0, 1):
            @pl.when(has_t[d])
            def _():
                pl.when(jnp.logical_not(is_inner & (off == d)))(lambda: t_in(j, d, 1).wait_recv())
                for e in (0, 1):
                    pl.when(has_h[e])(lambda: t_in(j, d, 2 * e).wait_recv())

        for k in (0, 1):
            queries = qb[j, k].reshape(3 * TILE, HEAD_DIM)
            keys = kv[j, k : k + 3, :, 0].reshape(9 * TILE, HEAD_DIM)
            values = kv[j, k : k + 3, :, 1].reshape(9 * TILE, HEAD_DIM)
            counted = valid[k : k + 3].reshape(9 * TILE, HEAD_DIM)
            scores = lax.dot_general(
                queries, keys, (((1,), (1,)), ((), ())), preferred_element_type=jnp.float32
            )
            highest = jnp.max(scores, axis=1, keepdims=True)
            weights = jnp.exp2((scores - highest) * SCALE).astype(jnp.bfloat16)
            blended = jnp.dot(
                weights, jnp.concatenate([values, counted], axis=1), preferred_element_type=jnp.float32
            )
            totals = blended[:, HEAD_DIM:]
            part = blended[:, :HEAD_DIM] / totals
            level = highest * SCALE + jnp.log2(totals)
            own_o[j, k] = part[TILE : 2 * TILE]
            own_l[j, k] = level[TILE : 2 * TILE]
            for d in (0, 1):
                at = slice(2 * d * TILE, (2 * d + 1) * TILE)
                osend[j, d, k] = part[at].astype(jnp.bfloat16)
                ssend[j, d, k : k + 1] = jnp.sum(jnp.where(diagonal, level[at], 0.0), axis=0, keepdims=True)
        for d in (0, 1):
            @pl.when(has_w[d])
            def _():
                o_copy(j, d).start()
                s_copy(j, d).start()

    def combine(j):
        for d in (0, 1):
            @pl.when(has_w[d])
            def _():
                o_in(j, d).wait_recv()
                s_in(j, d).wait_recv()
        for k in (0, 1):
            levels = [own_l[j, k]]
            for d in (0, 1):
                row = jnp.broadcast_to(srecv[j, d, k : k + 1], (TILE, HEAD_DIM))
                levels.append(jnp.sum(jnp.where(diagonal, row, 0.0), axis=1, keepdims=True))
            top = jnp.maximum(jnp.maximum(levels[1], levels[2]), levels[0])
            shares = [jnp.exp2(level - top) for level in levels]
            mixed = shares[0] * own_o[j, k]
            for d in (0, 1):
                mixed += shares[1 + d] * orecv[j, d, k].astype(jnp.float32)
            at = pl.ds(pl.multiple_of(j * HEAD_DIM, HEAD_DIM), HEAD_DIM)
            result = (mixed / (shares[0] + shares[1] + shares[2])).astype(jnp.bfloat16)
            outb[TT * k : TT * (k + 1), :, :, at] = result.reshape(TT, TH, TW, HEAD_DIM)

    @pl.loop(0, heads + BEHIND)
    def _(step):
        pl.when(step + AHEAD < heads)(lambda: launch(step + AHEAD))
        pl.when(step < heads)(lambda: forward(step))
        pl.when((step >= 1) & (step <= heads))(lambda: attend(step - 1))
        pl.when(step >= BEHIND)(lambda: combine(step - BEHIND))

    @pl.loop(0, heads)
    def _(j):
        pl.when(is_relay)(lambda: relay_out(j).wait_send())
        pl.when(is_inner & has_off)(lambda: edge_copy(j).wait_send())
        for d in (0, 1):
            @pl.when(far[d])
            def _():
                to_relay(j).wait_send()
                x_half(j, d).wait_send()

            pl.when(has_h[d] & jnp.logical_not(far[d]))(lambda: x_copy(j, d).wait_send())

            @pl.when(has_t[d])
            def _():
                t_copy(j, d, 1).wait_send()
                for e in (0, 1):
                    pl.when(has_h[e] & spreads(d, e))(lambda: t_copy(j, d, 2 * e).wait_send())

            @pl.when(has_w[d])
            def _():
                q_copy(j, d).wait_send()
                o_copy(j, d).wait_send()
                s_copy(j, d).wait_send()


def body(queries, keys, values):
    heads = queries.shape[3] // HEAD_DIM
    bf16, f32 = jnp.bfloat16, jnp.float32
    dma = pltpu.SemaphoreType.DMA
    own = pltpu.VMEM(queries.shape, jnp.bfloat16)
    return pl.pallas_call(
        functools.partial(kernel, heads),
        out_shape=jax.ShapeDtypeStruct(queries.shape, bf16),
        in_specs=[pl.BlockSpec(memory_space=pl.ANY)] * 3,
        out_specs=pl.BlockSpec(memory_space=pltpu.VMEM),
        scratch_shapes=[
            own, own, own,
            pltpu.VMEM((heads, 2, 3, TILE, HEAD_DIM), bf16),
            pltpu.VMEM((heads, 4, 3, 2, TILE, HEAD_DIM), bf16),
            pltpu.VMEM((4, 3, TILE, HEAD_DIM), bf16),
            pltpu.VMEM((heads, 2, 2, TILE, HEAD_DIM), bf16),
            pltpu.VMEM((heads, 2, 2, TILE, HEAD_DIM), bf16),
            pltpu.VMEM((heads, 2, 8, HEAD_DIM), f32),
            pltpu.VMEM((heads, 2, 8, HEAD_DIM), f32),
            pltpu.VMEM((heads, 2, TILE, HEAD_DIM), f32),
            pltpu.VMEM((heads, 2, TILE, HEAD_DIM), f32),
            pltpu.VMEM((heads, 2, TILE, HEAD_DIM), bf16),
            dma((3,)), dma((heads,)),
            dma((heads, 2)), dma((heads, 2)),
            dma((heads, 2, 3)), dma((heads, 2, 3)),
            dma((heads, 2)), dma((heads, 2)),
            dma((heads, 2)), dma((heads, 2)),
            dma((heads, 2)), dma((heads, 2)),
            dma((heads,)), dma((heads,)), dma((heads,)), dma((heads,)),
        ],
        compiler_params=pltpu.CompilerParams(
            collective_id=0, has_side_effects=True, vmem_limit_bytes=63 * 2**20
        ),
        name="window_attention",
    )(queries, keys, values)


def solution(mesh):
    placed = (P("ta", "ha", "wa", None),) * 3
    return jax.shard_map(
        body, mesh=mesh, in_specs=placed, out_specs=P("ta", "ha", "wa", None), check_vma=False
    )
```

time: 112 us -> 68.7 us (0.61)
  the two profiles are of different devices: /device:TPU:7 before, /device:TPU:215 now
where the time goes in v2:
time: 68.7 us; the launch traced here: 68.5 us
  Pallas kernels  66.4 us (97%)
  local copies, waits for them, and re-layouts  2.13 us (3%)
    pallas_call x1, Pallas kernels, body(): pl.pallas_call(functools.partial(kernel, heads), out_shape=jax.ShapeDtype...  66.4 us
    unnamed x1, local copies, waits for them, and re-layouts  2.13 us

profile of v2, /device:TPU:215, one launch (start us, length us, event | category | flops | bytes accessed | tf_op | source)
XLA Modules:
  0.0 68.5 jit_solution(4927426467947614225)
XLA Ops:
  0.0 66.4 %window_attention.1 = bf16[12,4,4,1536]{3,2,1,0:T(4,128)(2,1)} custom-call(bf16[12,4,4,1536]{3,2,1,0:T(4,128)(2,1)} %q_hbm.1, bf16[12,4,4,1536]{3,2,1,0:T(4,128)(2,1)} %k_hbm.1, bf16[12,4,4,1536]{3,2,1,0:T(4,128)(2,1)} %v_hbm.1), custom_call_target="tpu_custom_call" | custom-call | tf_op jit(solution)/shard_map/window_attention/pallas_call | solution.py:319
  66.4 2.1 %copy.5 = bf16[12,4,4,1536]{3,2,1,0:T(4,128)(2,1)} copy(bf16[12,4,4,1536]{3,2,1,0:T(4,128)(2,1)} %window_attention.1) | data formatting | bytes 1179648

commit v3 on v2

v3 whole, which is shorter than its diff:
```python
import functools
import math

import jax
import jax.numpy as jnp
from jax import lax
from jax.experimental import pallas as pl
from jax.experimental.pallas import tpu as pltpu
from jax.sharding import PartitionSpec as P

HEAD_DIM = 128
TT, TH, TW = 6, 4, 4
TILE = TT * TH * TW
MESH = pl.DeviceIdType.MESH
SCALE = HEAD_DIM**-0.5 * math.log2(math.e)
SHARES = (32, 32, 16, 16)
RELAYS = (0, 2, 1)
INNER = False
GROUP = 2
AHEAD = 2
FAR_AHEAD = 3
LEAD = 1
BEHIND = 3


def kernel(
    groups, q_hbm, k_hbm, v_hbm, outb,
    q_own, k_own, v_own, qb, kv, valid, osend, orecv, ssend, srecv, own_o, own_l,
    passing, load, es, xs, xr, ts, tr, qs, qr, os_, or_, ss, sr, ps, pr, fs, fr,
):
    t, h, w = lax.axis_index("ta"), lax.axis_index("ha"), lax.axis_index("wa")
    nt, nh, nw = lax.axis_size("ta"), lax.axis_size("ha"), lax.axis_size("wa")
    has_t = (t > 0, t < nt - 1)
    has_h = (h > 0, h < nh - 1)
    has_w = (w > 0, w < nw - 1)
    near_t = ((t - 1, h, w), (t + 1, h, w))
    near_h = ((t, h - 1, w), (t, h + 1, w))
    near_w = ((t, h, w - 1), (t, h, w + 1))
    low, high = nh // 2 - 1, nh // 2
    far = (h == high, h == low)
    is_far = (h == low) | (h == high)
    lower = h <= low
    relays = [(t, jnp.where(h == low, r, nh - 1 - r), w) for r in RELAYS]
    other_relays = [(t, jnp.where(h == low, nh - 1 - r, r), w) for r in RELAYS]
    is_relay = [(h == r) | (h == nh - 1 - r) for r in RELAYS]
    relay_from = (t, jnp.where(lower, low, high), w)
    relay_to = (t, jnp.where(lower, high, low), w)
    shares = [pl.ds(sum(SHARES[:i]), size) for i, size in enumerate(SHARES)]
    far_slot = jnp.where(h == low, 2, 0)
    relay_slot = jnp.where(lower, 0, 2)

    off = lax.rem(t, 2)
    has_off = (off == 0) & has_t[0] | (off == 1) & has_t[1]
    is_inner = (h == low - 1) | (h == high + 1)
    inner_slot = jnp.where(h == low - 1, 0, 2)
    inner_to = (t, jnp.where(h == low - 1, low, high), w)

    def remote(src, dst, send, recv, device):
        return pltpu.make_async_remote_copy(src, dst, send, recv, device_id=device, device_id_type=MESH)

    def nth(j):
        return 0 if isinstance(j, slice) else j

    def x_copy(j, d):
        return remote(kv.at[j, :, 1:3, 1], kv.at[j, :, 1:3, 0 if d else 2], xs.at[d], xr.at[nth(j), 1 - d], near_h[d])

    def x_half(j, d):
        return remote(
            kv.at[j, :, 1:3, 1, :, shares[0]], kv.at[j, :, 1:3, 0 if d else 2, :, shares[0]],
            xs.at[d], xr.at[nth(j), 1 - d], near_h[d],
        )

    def held(j, i):
        return passing.at[j, :, :, :, pl.ds(0, SHARES[1 + i])]

    def to_relay(j, i):
        return remote(kv.at[j, :, 1:3, 1, :, shares[1 + i]], held(j, i), ps.at[i], pr.at[nth(j)], relays[i])

    def relay_in(j, i):
        return remote(kv.at[j, :, 1:3, 1, :, shares[1 + i]], held(j, i), ps.at[i], pr.at[nth(j)], relay_from)

    def relay_out(j, i):
        return remote(
            held(j, i), kv.at[j, :, 1:3, relay_slot, :, shares[1 + i]], fs.at[i], fr.at[nth(j), i], relay_to
        )

    def from_relay(j, i):
        return remote(
            held(j, i), kv.at[j, :, 1:3, far_slot, :, shares[1 + i]], fs.at[i], fr.at[nth(j), i], other_relays[i]
        )

    def t_copy(j, d, hh):
        return remote(kv.at[j, :, 1 + d, hh], kv.at[j, :, 0 if d else 3, hh], ts.at[d, hh], tr.at[nth(j), 1 - d, hh], near_t[d])

    def edge_copy(j):
        return remote(
            kv.at[j, :, 3 * off, 1], kv.at[j, :, 3 * off, inner_slot], es.at[0], tr.at[nth(j), off, inner_slot], inner_to
        )

    def q_copy(j, d):
        return remote(qb.at[j, :, :, 1], qb.at[j, :, :, 0 if d else 2], qs.at[d], qr.at[nth(j), 1 - d], near_w[d])

    def o_copy(j, d):
        return remote(osend.at[j, d], orecv.at[j, 1 - d], os_.at[d], or_.at[nth(j), 1 - d], near_w[d])

    def s_copy(j, d):
        return remote(ssend.at[j, d], srecv.at[j, 1 - d], ss.at[d], sr.at[nth(j), 1 - d], near_w[d])

    def x_in(j, d):
        return remote(kv.at[j, :, 1:3, 1], kv.at[j, :, 1:3, 2 * d], xs.at[d], xr.at[nth(j), d], near_h[d])

    def x_half_in(j, d):
        return remote(
            kv.at[j, :, 1:3, 1, :, shares[0]], kv.at[j, :, 1:3, 2 * d, :, shares[0]],
            xs.at[d], xr.at[nth(j), d], near_h[d],
        )

    def t_in(j, d, hh):
        return remote(kv.at[j, :, 1 + d, 1], kv.at[j, :, 3 * d, hh], ts.at[d, hh], tr.at[nth(j), d, hh], (t + 2 * d - 1, h, w))

    def q_in(j, d):
        return remote(qb.at[j, :, :, 1], qb.at[j, :, :, 2 * d], qs.at[d], qr.at[nth(j), d], near_w[d])

    def o_in(j, d):
        return remote(osend.at[j, d], orecv.at[j, d], os_.at[d], or_.at[nth(j), d], near_w[d])

    def s_in(j, d):
        return remote(ssend.at[j, d], srecv.at[j, d], ss.at[d], sr.at[nth(j), d], near_w[d])

    loads = [
        pltpu.make_async_copy(src, dst, load.at[i])
        for i, (src, dst) in enumerate(((k_hbm, k_own), (v_hbm, v_own), (q_hbm, q_own)))
    ]
    for copy in loads:
        copy.start()

    barrier = pltpu.get_barrier_semaphore()
    count = jnp.int32(0)
    for has, near in ((has_t, near_t), (has_h, near_h), (has_w, near_w)):
        for d in (0, 1):
            pl.when(has[d])(
                lambda near=near, d=d: pl.semaphore_signal(
                    barrier, inc=1, device_id=near[d], device_id_type=MESH
                )
            )
            count += has[d].astype(jnp.int32)
    greet = [(is_far, r) for r in relays + other_relays]
    greet += [(here, near) for here in is_relay for near in (relay_from, relay_to)]
    for here, near in greet:
        pl.when(here)(
            lambda near=near: pl.semaphore_signal(barrier, inc=1, device_id=near, device_id_type=MESH)
        )
        count += here.astype(jnp.int32)

    for tt in range(4):
        for hh in range(3):
            here = jnp.bool_(True)
            if tt in (0, 3):
                here = here & has_t[tt // 3]
            if hh in (0, 2):
                here = here & has_h[hh // 2]
            valid[tt, hh] = jnp.full((TILE, HEAD_DIM), here.astype(jnp.float32)).astype(jnp.bfloat16)
    for d in (0, 1):
        @pl.when(jnp.logical_not(has_w[d]))
        def _():
            qb[:, :, :, 2 * d] = jnp.zeros_like(qb[:, :, :, 2 * d])
            orecv[:, d] = jnp.zeros_like(orecv[:, d])
            srecv[:, d] = jnp.full_like(srecv[:, d], -1e30)

    def tiles(ref, j):
        at = pl.ds(pl.multiple_of(j * HEAD_DIM, HEAD_DIM), HEAD_DIM)
        return ref[:, :, :, at].reshape(2, TILE, HEAD_DIM)

    for copy in loads:
        copy.wait()

    none = jnp.zeros((TILE, HEAD_DIM), jnp.bfloat16)

    @pl.loop(0, groups)
    def _(j):
        @pl.loop(0, GROUP)
        def _(g):
            kv[j, g, 1:3, 1, 0] = tiles(k_own, j * GROUP + g)
            kv[j, g, 1:3, 1, 1] = tiles(v_own, j * GROUP + g)
            qb[j, g, :, 1] = tiles(q_own, j * GROUP + g)
            for e in (0, 1):
                @pl.when(jnp.logical_not(has_h[e]))
                def _():
                    for tt in range(4):
                        kv[j, g, tt, 2 * e, 0] = kv[j, g, 1 + tt // 2, 1, 0]
                        kv[j, g, tt, 2 * e, 1] = none
            for d in (0, 1):
                @pl.when(jnp.logical_not(has_t[d]))
                def _():
                    for hh in range(3):
                        kv[j, g, 3 * d, hh, 0] = kv[j, g, 1 + d, 1, 0]
                        kv[j, g, 3 * d, hh, 1] = none

    pl.semaphore_wait(barrier, count)

    def launch_far(j):
        for d in (0, 1):
            @pl.when(far[d])
            def _():
                for i in range(len(RELAYS)):
                    to_relay(j, i).start()
                x_half(j, d).start()

    def launch(j):
        for d in (0, 1):
            pl.when(has_h[d] & jnp.logical_not(far[d]))(lambda: x_copy(j, d).start())
        for d in (0, 1):
            pl.when(has_t[d])(lambda: t_copy(j, d, 1).start())
        for d in (0, 1):
            pl.when(has_w[d])(lambda: q_copy(j, d).start())

    pl.loop(0, FAR_AHEAD)(launch_far)
    pl.loop(0, AHEAD)(launch)

    rows = lax.broadcasted_iota(jnp.int32, (TILE, HEAD_DIM), 0)
    lanes = lax.broadcasted_iota(jnp.int32, (TILE, HEAD_DIM), 1)
    diagonal = rows == lanes

    def spreads(d, e):
        return has_t[d] & jnp.logical_not((off == d) & far[1 - e]) if INNER else has_t[d]

    def pass_on(j):
        for i in range(len(RELAYS)):
            @pl.when(is_relay[i])
            def _():
                relay_in(j, i).wait_recv()
                relay_out(j, i).start()

    def forward(j):

        if INNER:
            @pl.when(is_inner & has_off)
            def _():
                t_in(j, off, 1).wait_recv()
                edge_copy(j).start()

        def spread(e):
            for d in (0, 1):
                pl.when(spreads(d, e))(lambda: t_copy(j, d, 2 * e).start())

        for e in (0, 1):
            @pl.when(has_h[e] & jnp.logical_not(far[e]))
            def _():
                x_in(j, e).wait_recv()
                spread(e)
        for e in (0, 1):
            @pl.when(far[e])
            def _():
                x_half_in(j, e).wait_recv()
                for i in range(len(RELAYS)):
                    from_relay(j, i).wait_recv()
                spread(e)

    def attend(j):
        for d in (0, 1):
            pl.when(has_w[d])(lambda: q_in(j, d).wait_recv())
        for d in (0, 1):
            @pl.when(has_t[d])
            def _():
                waits = jnp.logical_not(is_inner & (off == d)) if INNER else True
                pl.when(waits)(lambda: t_in(j, d, 1).wait_recv())
                for e in (0, 1):
                    pl.when(has_h[e])(lambda: t_in(j, d, 2 * e).wait_recv())

        @pl.loop(0, GROUP)
        def _(g):
            for k in (0, 1):
                queries = qb[j, g, k].reshape(3 * TILE, HEAD_DIM)
                keys = kv[j, g, k : k + 3, :, 0].reshape(9 * TILE, HEAD_DIM)
                values = kv[j, g, k : k + 3, :, 1].reshape(9 * TILE, HEAD_DIM)
                counted = valid[k : k + 3].reshape(9 * TILE, HEAD_DIM)
                scores = lax.dot_general(
                    queries, keys, (((1,), (1,)), ((), ())), preferred_element_type=jnp.float32
                )
                highest = jnp.max(scores, axis=1, keepdims=True)
                weights = jnp.exp2((scores - highest) * SCALE).astype(jnp.bfloat16)
                blended = jnp.dot(
                    weights, jnp.concatenate([values, counted], axis=1), preferred_element_type=jnp.float32
                )
                totals = blended[:, HEAD_DIM:]
                part = blended[:, :HEAD_DIM] / totals
                level = highest * SCALE + jnp.log2(totals)
                own_o[j, g, k] = part[TILE : 2 * TILE]
                own_l[j, g, k] = level[TILE : 2 * TILE]
                for d in (0, 1):
                    at = slice(2 * d * TILE, (2 * d + 1) * TILE)
                    osend[j, d, g, k] = part[at].astype(jnp.bfloat16)
                    ssend[j, d, g, k : k + 1] = jnp.sum(jnp.where(diagonal, level[at], 0.0), axis=0, keepdims=True)

        for d in (0, 1):
            @pl.when(has_w[d])
            def _():
                o_copy(j, d).start()
                s_copy(j, d).start()

    def combine(j):
        for d in (0, 1):
            @pl.when(has_w[d])
            def _():
                o_in(j, d).wait_recv()
                s_in(j, d).wait_recv()
        @pl.loop(0, GROUP)
        def _(g):
            for k in (0, 1):
                levels = [own_l[j, g, k]]
                for d in (0, 1):
                    row = jnp.broadcast_to(srecv[j, d, g, k : k + 1], (TILE, HEAD_DIM))
                    levels.append(jnp.sum(jnp.where(diagonal, row, 0.0), axis=1, keepdims=True))
                top = jnp.maximum(jnp.maximum(levels[1], levels[2]), levels[0])
                shares = [jnp.exp2(level - top) for level in levels]
                mixed = shares[0] * own_o[j, g, k]
                for d in (0, 1):
                    mixed += shares[1 + d] * orecv[j, d, g, k].astype(jnp.float32)
                at = pl.ds(pl.multiple_of((j * GROUP + g) * HEAD_DIM, HEAD_DIM), HEAD_DIM)
                result = (mixed / (shares[0] + shares[1] + shares[2])).astype(jnp.bfloat16)
                outb[TT * k : TT * (k + 1), :, :, at] = result.reshape(TT, TH, TW, HEAD_DIM)

    pl.loop(0, LEAD)(pass_on)

    @pl.loop(0, groups + BEHIND)
    def _(step):
        pl.when(step + FAR_AHEAD < groups)(lambda: launch_far(step + FAR_AHEAD))
        pl.when(step + LEAD < groups)(lambda: pass_on(step + LEAD))
        pl.when(step + AHEAD < groups)(lambda: launch(step + AHEAD))
        pl.when(step < groups)(lambda: forward(step))
        pl.when((step >= 1) & (step <= groups))(lambda: attend(step - 1))
        pl.when(step >= BEHIND)(lambda: combine(step - BEHIND))

    every = slice(None)
    for i in range(len(RELAYS)):
        pl.when(is_relay[i])(lambda: relay_out(every, i).wait_send())
    if INNER:
        pl.when(is_inner & has_off)(lambda: edge_copy(every).wait_send())
    for d in (0, 1):
        @pl.when(far[d])
        def _():
            for i in range(len(RELAYS)):
                to_relay(every, i).wait_send()
            x_half(every, d).wait_send()

        pl.when(has_h[d] & jnp.logical_not(far[d]))(lambda: x_copy(every, d).wait_send())

        @pl.when(has_t[d])
        def _():
            t_copy(every, d, 1).wait_send()
            for e in (0, 1):
                pl.when(has_h[e] & spreads(d, e))(lambda: t_copy(every, d, 2 * e).wait_send())

        @pl.when(has_w[d])
        def _():
            q_copy(every, d).wait_send()
            o_copy(every, d).wait_send()
            s_copy(every, d).wait_send()


def body(queries, keys, values):
    groups = queries.shape[3] // HEAD_DIM // GROUP
    bf16, f32 = jnp.bfloat16, jnp.float32
    dma = pltpu.SemaphoreType.DMA
    own = pltpu.VMEM(queries.shape, jnp.bfloat16)
    return pl.pallas_call(
        functools.partial(kernel, groups),
        out_shape=jax.ShapeDtypeStruct(queries.shape, bf16),
        in_specs=[pl.BlockSpec(memory_space=pl.ANY)] * 3,
        out_specs=pl.BlockSpec(memory_space=pltpu.VMEM),
        scratch_shapes=[
            own, own, own,
            pltpu.VMEM((groups, GROUP, 2, 3, TILE, HEAD_DIM), bf16),
            pltpu.VMEM((groups, GROUP, 4, 3, 2, TILE, HEAD_DIM), bf16),
            pltpu.VMEM((4, 3, TILE, HEAD_DIM), bf16),
            pltpu.VMEM((groups, 2, GROUP, 2, TILE, HEAD_DIM), bf16),
            pltpu.VMEM((groups, 2, GROUP, 2, TILE, HEAD_DIM), bf16),
            pltpu.VMEM((groups, 2, GROUP, 8, HEAD_DIM), f32),
            pltpu.VMEM((groups, 2, GROUP, 8, HEAD_DIM), f32),
            pltpu.VMEM((groups, GROUP, 2, TILE, HEAD_DIM), f32),
            pltpu.VMEM((groups, GROUP, 2, TILE, HEAD_DIM), f32),
            pltpu.VMEM((groups, GROUP, 2, 2, max(SHARES[1:]), HEAD_DIM), bf16),
            dma((3,)), dma((1,)),
            dma((2,)), dma((groups, 2)),
            dma((2, 3)), dma((groups, 2, 3)),
            dma((2,)), dma((groups, 2)),
            dma((2,)), dma((groups, 2)),
            dma((2,)), dma((groups, 2)),
            dma((len(RELAYS),)), dma((groups,)), dma((len(RELAYS),)), dma((groups, len(RELAYS))),
        ],
        compiler_params=pltpu.CompilerParams(
            collective_id=0, has_side_effects=True, vmem_limit_bytes=63 * 2**20
        ),
        name="window_attention",
    )(queries, keys, values)


def solution(mesh):
    placed = (P("ta", "ha", "wa", None),) * 3
    return jax.shard_map(
        body, mesh=mesh, in_specs=placed, out_specs=P("ta", "ha", "wa", None), check_vma=False
    )
```

time: 68.7 us -> 61.2 us (0.89)
  the two profiles are of different devices: /device:TPU:215 before, /device:TPU:199 now
where the time goes in v3:
time: 61.2 us; the launch traced here: 61 us
  Pallas kernels  58.9 us (96%)
  local copies, waits for them, and re-layouts  2.13 us (3%)
    pallas_call x1, Pallas kernels, body(): pl.pallas_call(functools.partial(kernel, groups), out_shape=jax.ShapeDtyp...  58.9 us
    unnamed x1, local copies, waits for them, and re-layouts  2.13 us

profile of v3, /device:TPU:199, one launch (start us, length us, event | category | flops | bytes accessed | tf_op | source)
XLA Modules:
  0.0 61.0 jit_solution(9474381149737808283)
XLA Ops:
  0.0 58.9 %window_attention.1 = bf16[12,4,4,1536]{3,2,1,0:T(4,128)(2,1)} custom-call(bf16[12,4,4,1536]{3,2,1,0:T(4,128)(2,1)} %q_hbm.1, bf16[12,4,4,1536]{3,2,1,0:T(4,128)(2,1)} %k_hbm.1, bf16[12,4,4,1536]{3,2,1,0:T(4,128)(2,1)} %v_hbm.1), custom_call_target="tpu_custom_call" | custom-call | tf_op jit(solution)/shard_map/window_attention/pallas_call | solution.py:366
  58.9 2.1 %copy.5 = bf16[12,4,4,1536]{3,2,1,0:T(4,128)(2,1)} copy(bf16[12,4,4,1536]{3,2,1,0:T(4,128)(2,1)} %window_attention.1) | data formatting | bytes 1179648

commit v4 on v3

--- a/solution.py
+++ b/solution.py
@@ -16,11 +16,11 @@
 SHARES = (32, 32, 16, 16)
 RELAYS = (0, 2, 1)
 INNER = False
-GROUP = 2
+GROUP = 3
 AHEAD = 2
 FAR_AHEAD = 3
 LEAD = 1
-BEHIND = 3
+BEHIND = 2
 
 
 def kernel(
@@ -100,11 +100,11 @@
     def q_copy(j, d):
         return remote(qb.at[j, :, :, 1], qb.at[j, :, :, 0 if d else 2], qs.at[d], qr.at[nth(j), 1 - d], near_w[d])
 
-    def o_copy(j, d):
-        return remote(osend.at[j, d], orecv.at[j, 1 - d], os_.at[d], or_.at[nth(j), 1 - d], near_w[d])
-
-    def s_copy(j, d):
-        return remote(ssend.at[j, d], srecv.at[j, 1 - d], ss.at[d], sr.at[nth(j), 1 - d], near_w[d])
+    def o_copy(j, d, g):
+        return remote(osend.at[j, d, g], orecv.at[j, 1 - d, g], os_.at[d], or_.at[nth(j), nth(g), 1 - d], near_w[d])
+
+    def s_copy(j, d, g):
+        return remote(ssend.at[j, d, g], srecv.at[j, 1 - d, g], ss.at[d], sr.at[nth(j), nth(g), 1 - d], near_w[d])
 
     def x_in(j, d):
         return remote(kv.at[j, :, 1:3, 1], kv.at[j, :, 1:3, 2 * d], xs.at[d], xr.at[nth(j), d], near_h[d])
@@ -121,11 +121,11 @@
     def q_in(j, d):
         return remote(qb.at[j, :, :, 1], qb.at[j, :, :, 2 * d], qs.at[d], qr.at[nth(j), d], near_w[d])
 
-    def o_in(j, d):
-        return remote(osend.at[j, d], orecv.at[j, d], os_.at[d], or_.at[nth(j), d], near_w[d])
-
-    def s_in(j, d):
-        return remote(ssend.at[j, d], srecv.at[j, d], ss.at[d], sr.at[nth(j), d], near_w[d])
+    def o_in(j, d, g):
+        return remote(osend.at[j, d, g], orecv.at[j, d, g], os_.at[d], or_.at[nth(j), nth(g), d], near_w[d])
+
+    def s_in(j, d, g):
+        return remote(ssend.at[j, d, g], srecv.at[j, d, g], ss.at[d], sr.at[nth(j), nth(g), d], near_w[d])
 
     loads = [
         pltpu.make_async_copy(src, dst, load.at[i])
@@ -291,21 +291,20 @@
                     at = slice(2 * d * TILE, (2 * d + 1) * TILE)
                     osend[j, d, g, k] = part[at].astype(jnp.bfloat16)
                     ssend[j, d, g, k : k + 1] = jnp.sum(jnp.where(diagonal, level[at], 0.0), axis=0, keepdims=True)
-
-        for d in (0, 1):
-            @pl.when(has_w[d])
-            def _():
-                o_copy(j, d).start()
-                s_copy(j, d).start()
+            for d in (0, 1):
+                @pl.when(has_w[d])
+                def _():
+                    o_copy(j, d, g).start()
+                    s_copy(j, d, g).start()
 
     def combine(j):
-        for d in (0, 1):
-            @pl.when(has_w[d])
-            def _():
-                o_in(j, d).wait_recv()
-                s_in(j, d).wait_recv()
         @pl.loop(0, GROUP)
         def _(g):
+            for d in (0, 1):
+                @pl.when(has_w[d])
+                def _():
+                    o_in(j, d, g).wait_recv()
+                    s_in(j, d, g).wait_recv()
             for k in (0, 1):
                 levels = [own_l[j, g, k]]
                 for d in (0, 1):
@@ -354,8 +353,8 @@
         @pl.when(has_w[d])
         def _():
             q_copy(every, d).wait_send()
-            o_copy(every, d).wait_send()
-            s_copy(every, d).wait_send()
+            o_copy(every, d, every).wait_send()
+            s_copy(every, d, every).wait_send()
 
 
 def body(queries, keys, values):
@@ -384,12 +383,12 @@
             dma((2,)), dma((groups, 2)),
             dma((2, 3)), dma((groups, 2, 3)),
             dma((2,)), dma((groups, 2)),
-            dma((2,)), dma((groups, 2)),
-            dma((2,)), dma((groups, 2)),
+            dma((2,)), dma((groups, GROUP, 2)),
+            dma((2,)), dma((groups, GROUP, 2)),
             dma((len(RELAYS),)), dma((groups,)), dma((len(RELAYS),)), dma((groups, len(RELAYS))),
         ],
         compiler_params=pltpu.CompilerParams(
-            collective_id=0, has_side_effects=True, vmem_limit_bytes=63 * 2**20
+            collective_id=0, has_side_effects=True, vmem_limit_bytes=53 * 2**20 + 2**17
         ),
         name="window_attention",
     )(queries, keys, values)

time: 61.2 us -> 58.5 us (0.956)
  Pallas kernels: 58.9 us -> 57.5 us
  local copies, waits for them, and re-layouts: 2.13 us -> 0.82 us
    pallas_call x1, Pallas kernels: 58.9 us -> 57.5 us  [body(): pl.pallas_call(functools.partial(kernel, groups), out_shape=jax.ShapeDtyp...]
    unnamed x1, local copies, waits for them, and re-layouts: 2.13 us -> 0.82 us
where the time goes in v4:
time: 58.5 us; the launch traced here: 58.3 us
  Pallas kernels  57.5 us (98%)
  local copies, waits for them, and re-layouts  0.82 us (1%)
    pallas_call x1, Pallas kernels, body(): pl.pallas_call(functools.partial(kernel, groups), out_shape=jax.ShapeDtyp...  57.5 us

profile of v4, /device:TPU:199, one launch (start us, length us, event | category | flops | bytes accessed | tf_op | source)
XLA Modules:
  0.0 58.3 jit_solution(15665593120057032672)
XLA Ops:
  0.0 57.5 %window_attention.1 = bf16[12,4,4,1536]{3,2,1,0:T(4,128)(2,1)S(1)} custom-call(bf16[12,4,4,1536]{3,2,1,0:T(4,128)(2,1)} %q_hbm.1, bf16[12,4,4,1536]{3,2,1,0:T(4,128)(2,1)} %k_hbm.1, bf16[12,4,4,1536]{3,2,1,0:T(4,128)(2,1)} %v_hbm.1), custom_call_target="tpu_custom_call" | custom-call | tf_op jit(solution)/shard_map/window_attention/pallas_call | solution.py:365
  57.5 0.8 %copy.5 = bf16[12,4,4,1536]{3,2,1,0:T(4,128)(2,1)} copy(bf16[12,4,4,1536]{3,2,1,0:T(4,128)(2,1)S(1)} %window_attention.1) | data formatting | bytes 1179648

commit v5 on v4

--- a/solution.py
+++ b/solution.py
@@ -17,8 +17,8 @@
 RELAYS = (0, 2, 1)
 INNER = False
 GROUP = 3
-AHEAD = 2
-FAR_AHEAD = 3
+AHEAD = 3
+FAR_AHEAD = 4
 LEAD = 1
 BEHIND = 2
 

time: 58.5 us -> 58.1 us (level)
  the two profiles are of different devices: /device:TPU:199 before, /device:TPU:197 now
where the time goes in v5:
time: 58.1 us; the launch traced here: 58 us
  Pallas kernels  57.1 us (98%)
  local copies, waits for them, and re-layouts  0.82 us (1%)
    pallas_call x1, Pallas kernels, body(): pl.pallas_call(functools.partial(kernel, groups), out_shape=jax.ShapeDtyp...  57.1 us

profile of v5, /device:TPU:197, one launch (start us, length us, event | category | flops | bytes accessed | tf_op | source)
XLA Modules:
  0.0 58.0 jit_solution(17463873411784065369)
XLA Ops:
  0.0 57.1 %window_attention.1 = bf16[12,4,4,1536]{3,2,1,0:T(4,128)(2,1)S(1)} custom-call(bf16[12,4,4,1536]{3,2,1,0:T(4,128)(2,1)} %q_hbm.1, bf16[12,4,4,1536]{3,2,1,0:T(4,128)(2,1)} %k_hbm.1, bf16[12,4,4,1536]{3,2,1,0:T(4,128)(2,1)} %v_hbm.1), custom_call_target="tpu_custom_call" | custom-call | tf_op jit(solution)/shard_map/window_attention/pallas_call | solution.py:365
  57.2 0.8 %copy.5 = bf16[12,4,4,1536]{3,2,1,0:T(4,128)(2,1)} copy(bf16[12,4,4,1536]{3,2,1,0:T(4,128)(2,1)S(1)} %window_attention.1) | data formatting | bytes 1179648
